TPU v7x, 256 devices: a whole 4x4x8 slice. The times are simulated.
256 devices in a mesh: inner: 8 (over y, z_hi), outer: 32 (over z_lo, x, core).
Axes of the slice: x: 4, y: 4, z: 8 (z_hi: 2, z_lo: 4; z = z_hi * 4 + z_lo), core: 2. Of those that a mesh axis runs over, the one named last changes fastest.
Arguments:
- queries: bfloat16 [2, 32, 8, 64, 4, 128], P(None, 'outer', 'inner'), may hold values from -20 to 20
- key_maps: bfloat16 [2, 32, 8, 64, 128], P(None, 'outer', 'inner'), may hold values from -20 to 20
- values: bfloat16 [2, 32, 8, 64, 128], P(None, 'outer', 'inner'), may hold values from -6 to 6
- lambdas: float32 [4], replicated, may hold values from 0.2 to 0.7
- norm_gain: float32 [128], replicated, may hold values from 0.1 to 1.9
- out_grad: bfloat16 [2, 32, 8, 64, 4, 128], P(None, 'outer', 'inner'), may hold values from -6 to 6
Outputs:
- attended: bfloat16 [2, 32, 8, 64, 4, 128], P(None, 'outer', 'inner')
- query_grad: bfloat16 [2, 32, 8, 64, 4, 128], P(None, 'outer', 'inner')
All inputs are finite; a program needn't handle non-finite values.
Results may differ from a plain program's by a relative error of at most 0.024.
Values may be sent and summed in bfloat16 or wider, within the bound.
A program may use at most 128 MiB of HBM per device.

v0:
```python
import math

import jax
import jax.numpy as jnp
from jax import lax
from jax.sharding import PartitionSpec as P

lam_init = 0.8 - 0.6 * math.exp(-3.3)
norm_eps = 1e-05
far_below = -1e30


def contract(left_op, right_op):
    return lax.dot_general(
        left_op, right_op, (((1,), (1,)), ((), ())), preferred_element_type=jnp.float32
    )


def absorb(run_top, run_sum, run_acc, scores, visible, vblock):
    new_top = jnp.maximum(run_top, jnp.max(jnp.where(visible, scores, far_below), axis=1))
    weights = jnp.exp(jnp.where(visible, scores - new_top[:, None], far_below))
    shrink = jnp.exp(run_top - new_top)
    run_sum = run_sum * shrink + jnp.sum(weights, axis=1)
    run_acc = run_acc * shrink[:, None] + jnp.dot(
        weights.astype(jnp.bfloat16), vblock, preferred_element_type=jnp.float32
    )
    return (new_top, run_sum, run_acc)


def forward_block(running, qblock, query_pos, kblock, vblock, key_pos, score_scale):
    map_width = kblock.shape[1] // 2
    visible = key_pos[None, :] <= query_pos[:, None]
    first_map = contract(qblock[:, :map_width], kblock[:, :map_width]) * score_scale
    second_map = contract(qblock[:, map_width:], kblock[:, map_width:]) * score_scale
    part_one = absorb(running[0], running[1], running[2], first_map, visible, vblock)
    part_two = absorb(running[3], running[4], running[5], second_map, visible, vblock)
    return part_one + part_two


def finish_forward(running, lambdas, norm_gain, grad_block, out_scale):
    top_one, sum_one, acc_one, top_two, sum_two, acc_two = running
    row_count = sum_one.shape[0]
    head_count = lambdas.shape[0]
    tok_count = row_count // head_count
    vwidth = acc_one.shape[1]
    out_one = (acc_one / sum_one[:, None]).reshape(tok_count, head_count, vwidth)
    out_two = (acc_two / sum_two[:, None]).reshape(tok_count, head_count, vwidth)
    lam_col = lambdas[None, :, None]
    differ = out_one - lam_col * out_two
    inv_rms = lax.rsqrt(jnp.mean(differ * differ, axis=-1, keepdims=True) + norm_eps)
    attended = (out_scale * norm_gain * differ * inv_rms).astype(jnp.bfloat16)
    scaled_grad = grad_block.astype(jnp.float32) * (out_scale * norm_gain)
    d_differ = inv_rms * scaled_grad - differ * inv_rms**3 * jnp.mean(
        scaled_grad * differ, axis=-1, keepdims=True
    )
    dot_one = jnp.sum(d_differ * out_one, axis=-1).reshape(row_count)
    dot_two = jnp.sum(d_differ * out_two, axis=-1).reshape(row_count)
    lse_one = top_one + jnp.log(sum_one)
    lse_two = top_two + jnp.log(sum_two)
    lam_rows = jnp.tile(lambdas, tok_count)
    back_rows = d_differ.reshape(row_count, vwidth).astype(jnp.bfloat16)
    return (attended, (lse_one, lse_two, dot_one, dot_two, lam_rows, back_rows))


def backward_block(grad_pair, qblock, query_pos, kblock, vblock, key_pos, score_scale, saved_stats):
    lse_one, lse_two, dot_one, dot_two, lam_rows, back_rows = saved_stats
    map_width = kblock.shape[1] // 2
    visible = key_pos[None, :] <= query_pos[:, None]
    first_map = contract(qblock[:, :map_width], kblock[:, :map_width]) * score_scale
    second_map = contract(qblock[:, map_width:], kblock[:, map_width:]) * score_scale
    prob_one = jnp.exp(jnp.where(visible, first_map - lse_one[:, None], far_below))
    prob_two = jnp.exp(jnp.where(visible, second_map - lse_two[:, None], far_below))
    through = contract(back_rows, vblock)
    slope_one = (prob_one * (through - dot_one[:, None])).astype(jnp.bfloat16)
    slope_two = (-lam_rows[:, None] * prob_two * (through - dot_two[:, None])).astype(jnp.bfloat16)
    grad_one = grad_pair[0] + jnp.dot(
        slope_one, kblock[:, :map_width], preferred_element_type=jnp.float32
    )
    grad_two = grad_pair[1] + jnp.dot(
        slope_two, kblock[:, map_width:], preferred_element_type=jnp.float32
    )
    return (grad_one, grad_two)


def lower_places(start_at, length, half_len, tok_total):
    return start_at + jnp.arange(length, dtype=jnp.int32)


def upper_places(start_at, length, half_len, tok_total):
    flat_idx = start_at + jnp.arange(length, dtype=jnp.int32)
    return tok_total - (flat_idx // half_len + 1) * half_len + flat_idx % half_len


def run_sweep(
    step_fn,
    running,
    key_seg,
    value_seg,
    placer,
    lower_turn,
    upper_turn,
    block_len,
    half_len,
    tok_total,
):

    def one_turn(turn_id, carried):
        kblock = lax.dynamic_slice_in_dim(key_seg, turn_id * block_len, block_len, 0)
        vblock = lax.dynamic_slice_in_dim(value_seg, turn_id * block_len, block_len, 0)
        key_pos = placer(turn_id * block_len, block_len, half_len, tok_total)
        return step_fn(carried, kblock, vblock, key_pos)

    return lax.fori_loop(lower_turn, upper_turn, one_turn, running)


def split_segments(key_whole, value_whole):
    span_len = key_whole.shape[1] * key_whole.shape[2] * key_whole.shape[3]
    lower_keys = key_whole[0].reshape(span_len, key_whole.shape[4])
    upper_keys = key_whole[1].reshape(span_len, key_whole.shape[4])
    lower_vals = value_whole[0].reshape(span_len, value_whole.shape[4])
    upper_vals = value_whole[1].reshape(span_len, value_whole.shape[4])
    return (lower_keys, lower_vals, upper_keys, upper_vals)


def body(queries, key_maps, values, lambdas, norm_gain, out_grad):
    half_len = queries.shape[3]
    head_count = queries.shape[4]
    map_width = queries.shape[5] // 2
    value_width = values.shape[4]
    inner_size = lax.axis_size("inner")
    outer_size = lax.axis_size("outer")
    span_len = inner_size * outer_size * half_len
    tok_total = 2 * span_len
    block_len = min(1024, span_len)
    score_scale = 1.0 / math.sqrt(map_width)
    out_scale = 1.0 - lam_init
    row_count = half_len * head_count
    own_block = lax.axis_index("outer") * inner_size + lax.axis_index("inner")
    row_tokens = jnp.arange(row_count, dtype=jnp.int32) // head_count
    low_pos = own_block * half_len + row_tokens
    high_pos = tok_total - (own_block + 1) * half_len + row_tokens
    low_query = queries[0, 0, 0].reshape(row_count, 2 * map_width)
    high_query = queries[1, 0, 0].reshape(row_count, 2 * map_width)
    empty_state = (
        jnp.full((row_count,), far_below, jnp.float32),
        jnp.zeros((row_count,), jnp.float32),
        jnp.zeros((row_count, value_width), jnp.float32),
    ) * 2
    low_end = (own_block * half_len + half_len + block_len - 1) // block_len
    high_start = own_block * half_len // block_len
    all_turns = span_len // block_len

    def low_step(running, kblock, vblock, key_pos):
        return forward_block(running, low_query, low_pos, kblock, vblock, key_pos, score_scale)

    def high_step(running, kblock, vblock, key_pos):
        return forward_block(running, high_query, high_pos, kblock, vblock, key_pos, score_scale)

    near_keys, near_values = (
        lax.all_gather(key_maps, "inner", axis=2, tiled=True),
        lax.all_gather(values, "inner", axis=2, tiled=True),
    )
    key_whole, value_whole = (
        lax.all_gather(near_keys, "outer", axis=1, tiled=True),
        lax.all_gather(near_values, "outer", axis=1, tiled=True),
    )
    segments = split_segments(key_whole, value_whole)
    lower_keys, lower_vals, upper_keys, upper_vals = segments
    low_run = run_sweep(
        low_step,
        empty_state,
        lower_keys,
        lower_vals,
        lower_places,
        0,
        low_end,
        block_len,
        half_len,
        tok_total,
    )
    high_run = run_sweep(
        high_step,
        empty_state,
        lower_keys,
        lower_vals,
        lower_places,
        0,
        all_turns,
        block_len,
        half_len,
        tok_total,
    )
    high_run = run_sweep(
        high_step,
        high_run,
        upper_keys,
        upper_vals,
        upper_places,
        high_start,
        all_turns,
        block_len,
        half_len,
        tok_total,
    )
    lower_keys, lower_vals, upper_keys, upper_vals = segments
    low_att, low_saved = finish_forward(low_run, lambdas, norm_gain, out_grad[0, 0, 0], out_scale)
    high_att, high_saved = finish_forward(
        high_run, lambdas, norm_gain, out_grad[1, 0, 0], out_scale
    )
    zero_grads = (jnp.zeros((row_count, map_width), jnp.float32),) * 2

    def low_back(grad_pair, kblock, vblock, key_pos):
        return backward_block(
            grad_pair, low_query, low_pos, kblock, vblock, key_pos, score_scale, low_saved
        )

    def high_back(grad_pair, kblock, vblock, key_pos):
        return backward_block(
            grad_pair, high_query, high_pos, kblock, vblock, key_pos, score_scale, high_saved
        )

    low_grads = run_sweep(
        low_back,
        zero_grads,
        lower_keys,
        lower_vals,
        lower_places,
        0,
        low_end,
        block_len,
        half_len,
        tok_total,
    )
    high_grads = run_sweep(
        high_back,
        zero_grads,
        lower_keys,
        lower_vals,
        lower_places,
        0,
        all_turns,
        block_len,
        half_len,
        tok_total,
    )
    high_grads = run_sweep(
        high_back,
        high_grads,
        upper_keys,
        upper_vals,
        upper_places,
        high_start,
        all_turns,
        block_len,
        half_len,
        tok_total,
    )

    def to_output(grad_pair):
        merged = jnp.concatenate(grad_pair, axis=1) * score_scale
        return merged.astype(jnp.bfloat16).reshape(half_len, head_count, 2 * map_width)

    attended = jnp.stack([low_att, high_att])[:, None, None]
    query_grad = jnp.stack([to_output(low_grads), to_output(high_grads)])[:, None, None]
    return (attended, query_grad)


def solution(mesh):
    in_specs = (
        P(None, "outer", "inner", None, None, None),
        P(None, "outer", "inner", None, None),
        P(None, "outer", "inner", None, None),
        P(),
        P(),
        P(None, "outer", "inner", None, None, None),
    )
    out_specs = (
        P(None, "outer", "inner", None, None, None),
        P(None, "outer", "inner", None, None, None),
    )
    return jax.shard_map(body, mesh=mesh, in_specs=in_specs, out_specs=out_specs, check_vma=False)
```

profile of v0, /device:TPU:1, one launch (start us, length us, event | category | flops | bytes accessed | tf_op | source)
XLA Modules:
  0.0 592.6 jit_solution(6379994108670687012)
XLA Ops:
  7.2 43.7 %all_gather.12 = bf16[2,1,8,64,128]{4,3,2,1,0:T(8,128)(2,1)} all-gather(bf16[2,1,1,64,128]{4,3,2,1,0:T(8,128)(2,1)} %param.19), channel_id=1, replica_groups=mesh['inner'=8,'outer'=32] {'inner'}, dimensions={2}, use_global_device_ids=true | all-gather | bytes 294912 | tf_op jit(solution)/shard_map/all_gather | solution.py:160
  51.0 41.8 %all_gather.14 = bf16[2,1,8,64,128]{4,3,2,1,0:T(8,128)(2,1)} all-gather(bf16[2,1,1,64,128]{4,3,2,1,0:T(8,128)(2,1)} %param.20), channel_id=1, replica_groups=mesh['inner'=8,'outer'=32] {'inner'}, dimensions={2}, use_global_device_ids=true | all-gather | bytes 294912 | tf_op jit(solution)/shard_map/all_gather | solution.py:161
  96.8 34.6 %all-gather.3.cloned.1.call-done = bf16[2,32,8,64,128]{4,3,2,1,0:T(8,128)(2,1)} async-done(((bf16[2,1,8,64,128]{4,3,2,1,0:T(8,128)(2,1)}), bf16[2,32,8,64,128]{4,3,2,1,0:T(8,128)(2,1)}) %all-gather.3.cloned.1.call-update) | async-done | bytes 8388624 | tf_op jit(solution)/shard_map/all_gather | solution.py:164
  131.4 7.3 %fusion.299 = (bf16[1,32,8,64,128]{4,3,2,1,0:T(8,128)(2,1)}, bf16[1,32,8,64,128]{4,3,2,1,0:T(8,128)(2,1)}) fusion(bf16[2,32,8,64,128]{4,3,2,1,0:T(8,128)(2,1)} %all-gather.3.cloned.1.call-done), kind=kLoop, calls=%fused_computation.392 | loop fusion | bytes 16777216 | tf_op jit(solution)/shard_map/slice | solution.py:119
  138.8 63.2 %all-gather.5.cloned.1.call-done = bf16[2,32,8,64,128]{4,3,2,1,0:T(8,128)(2,1)} async-done(((bf16[2,1,8,64,128]{4,3,2,1,0:T(8,128)(2,1)}), bf16[2,32,8,64,128]{4,3,2,1,0:T(8,128)(2,1)}) %all-gather.5.cloned.1.call-update) | async-done | bytes 8388624 | tf_op jit(solution)/shard_map/all_gather | solution.py:165
  202.0 7.3 %fusion.298 = (bf16[1,32,8,64,128]{4,3,2,1,0:T(8,128)(2,1)}, bf16[1,32,8,64,128]{4,3,2,1,0:T(8,128)(2,1)}) fusion(bf16[2,32,8,64,128]{4,3,2,1,0:T(8,128)(2,1)} %all-gather.5.cloned.1.call-done), kind=kLoop, calls=%fused_computation.391 | loop fusion | bytes 16777216 | tf_op jit(solution)/shard_map/slice | solution.py:121
  209.4 6.3 %while.119 = (s32[]{:T(128)}, f32[256]{0:T(256)S(1)}, f32[256]{0:T(256)S(1)}, f32[256,128]{1,0:T(8,128)S(1)}, f32[256]{0:T(256)S(1)}, /*index=5*/f32[256]{0:T(25...) while((s32[]{:T(128)}, f32[256]{0:T(256)S(1)}, ...), condition=%wide.region_5.6_spmd.clone, body=%wide.region_0.5_spmd.clone.sunk | while | flops 207229184 | bytes 9102579 | solution.py:113
  215.7 100.3 %while.121 = (s32[]{:T(128)}, f32[256]{0:T(256)S(1)}, f32[256]{0:T(256)S(1)}, f32[256,128]{1,0:T(8,128)S(1)}, f32[256]{0:T(256)S(1)}, /*index=5*/f32[256]{0:T(25...) while((s32[]{:T(128)}, f32[256]{0:T(256)S(1)}, ...), condition=%wide.region_12.13_spmd.clone, body=%wide.region_7.12_spmd.clone.sunk | while | flops 207296256 | bytes 9102585 | solution.py:113
  316.1 101.4 %while.120 = (s32[]{:T(128)}, f32[256]{0:T(256)S(1)}, f32[256]{0:T(256)S(1)}, f32[256,128]{1,0:T(8,128)S(1)}, f32[256]{0:T(256)S(1)}, /*index=5*/f32[256]{0:T(25...) while((s32[]{:T(128)}, f32[256]{0:T(256)S(1)}, ...), condition=%wide.region_18.19_spmd.clone, body=%wide.region_13.18_spmd.clone.sunk | while | flops 207252736 | bytes 9102571 | solution.py:113
  420.8 4.9 while.122
  425.9 78.8 %while.124 = (s32[]{:T(128)}, f32[256,64]{0,1:T(8,128)S(1)}, f32[256,64]{0,1:T(8,128)S(1)}, bf16[16384,128]{1,0:T(8,128)(2,1)}, bf16[256,128]{1,0:T(8,128)(2,1)S...) while((s32[]{:T(128)}, f32[256,64]{0,1:T(8,128)S(1)}, ...), condition=%wide.wide.region_29.30_spmd.clone, body=%wide.wide.region_28.29_spmd.clone.sunk | while | flops 205327616 | bytes 4943124 | solution.py:113
  427.3 1.8 fusion.482
  432.2 1.8 fusion.482
  437.1 1.8 fusion.482
  442.1 1.8 fusion.482
  447.0 1.8 fusion.482
  451.9 1.8 fusion.482
  456.8 1.8 fusion.482
  461.8 1.8 fusion.482
  466.7 1.8 fusion.482
  471.6 1.8 fusion.482
  486.4 1.8 fusion.482
  504.7 78.8 %while.123 = (s32[]{:T(128)}, f32[256,64]{0,1:T(8,128)S(1)}, f32[256,64]{0,1:T(8,128)S(1)}, bf16[16384,128]{1,0:T(8,128)(2,1)}, bf16[256,128]{1,0:T(8,128)(2,1)S...) while((s32[]{:T(128)}, f32[256,64]{0,1:T(8,128)S(1)}, ...), condition=%wide.wide.region_31.32_spmd.clone, body=%wide.wide.region_30.31_spmd.clone.sunk | while | flops 205318400 | bytes 4942091 | solution.py:113
  575.1 1.8 fusion.470
  (683 shorter events, 352.9 us)
Async XLA Ops:
  7.2 124.3 %all-gather.3.cloned.1.call-start = ((), (), s32[]{:S(2)}) async-start(), calls=%async_computation | async-start | bytes 8650752 | tf_op jit(solution)/shard_map/all_gather | solution.py:164
  50.9 151.1 %all-gather.5.cloned.1.call-start = ((), (), s32[]{:S(2)}) async-start(), calls=%async_computation.1 | async-start | bytes 8650752 | tf_op jit(solution)/shard_map/all_gather | solution.py:165
  316.0 101.8 %copy-start = (bf16[2,1,1,64,4,128]{5,4,3,2,1,0:T(4,128)(2,1)S(1)}, bf16[2,1,1,64,4,128]{5,4,3,2,1,0:T(4,128)(2,1)}, u32[]{:S(2)}) copy-start(bf16[2,1,1,64,4,128]{5,4,3,2,1,0:T(4,128)(2,1)} %param.23) | copy-start | bytes 393220
  316.1 101.8 %copy-start.5 = (f32[4]{0:T(128)S(1)}, f32[4]{0:T(128)}, u32[]{:S(2)}) copy-start(f32[4]{0:T(128)} %param.21) | copy-start | bytes 52
  419.0 1.7 copy-start.1
  419.4 1.4 copy-start.2
  419.9 0.6 copy-start.3
  420.1 0.6 copy-start.4
Sparse Core Ops, SparseCore 0:
  51.1 80.3 all-gather.2
  133.3 68.6 all-gather.4
where the time goes:
time: 599 us; the launch traced here: 593 us
  matrix products  345 us (58%)
  waiting for transfers between devices  97.9 us (16%)
  blocking collectives  85.5 us (14%)
  other arithmetic  22.3 us (4%)
  local copies, waits for them, and re-layouts  22.3 us (4%)
  between operations  14.5 us (2%)
    dot_general x99, matrix products, contract(): lax.dot_general(left_op, right_op, (((1,), (1,)), ((), ())), preferred_el...  128 us
    dot_general x66, matrix products, absorb(): jnp.dot(weights.astype(jnp.bfloat16), vblock, preferred_element_type=jnp....  101 us
    all_gather x1, waiting for transfers between devices, body(): lax.all_gather(near_values, 'outer', axis=1, tiled=True)  63.2 us
    dot_general x33, matrix products, backward_block(): jnp.dot(slope_two, kblock[:, map_width:], preferred_element_type=jnp.floa...  60.4 us
    dot_general x33, matrix products, backward_block(): jnp.dot(slope_one, kblock[:, :map_width], preferred_element_type=jnp.floa...  55.2 us
    all_gather x1, blocking collectives, body(): lax.all_gather(key_maps, 'inner', axis=2, tiled=True)  43.7 us
    all_gather x1, blocking collectives, body(): lax.all_gather(values, 'inner', axis=2, tiled=True)  41.8 us
    all_gather x1, waiting for transfers between devices, body(): lax.all_gather(near_keys, 'outer', axis=1, tiled=True)  34.6 us
  transfers between devices with their start and end apart: 2, of which 2 were waited for; matrix products, arithmetic and copies ran while one was open for 2% of the time, Pallas kernels for 0%

commit v1 on v0

v1 whole, which is shorter than its diff:
```python
import math

import jax
import jax.numpy as jnp
from jax import lax
from jax.experimental import pallas as pl
from jax.experimental.pallas import tpu as pltpu
from jax.sharding import PartitionSpec as P

lam_init = 0.8 - 0.6 * math.exp(-3.3)
OUT = 1.0 - lam_init
EPS = 1e-5
NEG = -1e30
F32, BF = jnp.float32, jnp.bfloat16
R = 256
CH = 512
MESH = pl.DeviceIdType.MESH


def nt(a, b):
    return lax.dot_general(a, b, (((1,), (1,)), ((), ())), preferred_element_type=F32)


def tn(a, b):
    return lax.dot_general(a, b, (((0,), (0,)), ((), ())), preferred_element_type=F32)


def device_at(x, y, z, core):
    return (y * 2 + z // 4, ((z % 4) * 4 + x) * 2 + core)


def kernel(
    q_ref, k_ref, v_ref, lam_ref, gain_ref, og_ref, att_ref, qg_ref,
    kv, w, qm, top, tot, acc, tops, back, dots, grads,
    zs, zr, s1, r1, s2, r2, ss, sr,
):
    inner, outer = lax.axis_index("inner"), lax.axis_index("outer")
    y, z = inner // 2, (inner % 2) * 4 + outer // 8
    x, core = (outer // 2) % 4, outer % 2
    first = core == 0
    a_pos, b_pos = jnp.where(first, x, y), jnp.where(first, y, x)

    def place(a, b):
        return jnp.where(first, a, b), jnp.where(first, b, a)

    def plane_device(da, db):
        px, py = place((a_pos + da) % 4, (b_pos + db) % 4)
        return device_at(px, py, z, core)

    up, down = device_at(x, y, (z + 1) % 8, core), device_at(x, y, (z + 7) % 8, core)
    sibling = device_at(x, y, z, 1 - core)

    def unit_z(k):
        half = (k + 1) // 2
        return (z + jnp.where(k % 2 == 1, half, 8 - half)) % 8

    def piece(k, da, db):
        px, py = place((a_pos + da) % 4, (b_pos + db) % 4)
        return kv.at[unit_z(k), px, core, py]

    def send(ref, send_sem, recv_sem, device):
        return pltpu.make_async_remote_copy(
            src_ref=ref, dst_ref=ref, send_sem=send_sem, recv_sem=recv_sem,
            device_id=device, device_id_type=MESH,
        )

    def z_copy(k, unit, device):
        return send(piece(k, 0, 0), zs.at[unit], zr.at[unit], device)

    def one_copy(k, slot):
        sign = 1 - 2 * (k % 2)
        if slot == 2:
            return send(piece(k, 4 - sign, 0), s1.at[k, 2], r1.at[k, 2], plane_device(4 + sign, 0))
        return send(piece(k, 0, 0), s1.at[k, slot], r1.at[k, slot], plane_device((1, 3)[slot], 0))

    def one_wait(k, slot):
        send(piece(k, (3, 1, 2)[slot], 0), s1.at[k, slot], r1.at[k, slot], sibling).wait_recv()

    SIDE = (0, 3, 1, 2)

    def two_copy(k, m, slot):
        if slot == 2:
            sign = (1, 3)[m % 2]
            return send(piece(k, SIDE[m], 4 - sign), s2.at[k, m, 2], r2.at[k, m, 2], plane_device(0, sign))
        return send(piece(k, SIDE[m], 0), s2.at[k, m, slot], r2.at[k, m, slot], plane_device(0, (1, 3)[slot]))

    def two_wait(k, m, slot):
        send(piece(k, SIDE[m], (3, 1, 2)[slot]), s2.at[k, m, slot], r2.at[k, m, slot], sibling).wait_recv()

    def pair_copy(k, mine):
        ref = kv.at[unit_z(k), :, core if mine else 1 - core]
        return send(ref, ss.at[k], sr.at[k], sibling)

    for c in range(2):
        kv[z, x, core, y, c, 0] = k_ref[c]
        kv[z, x, core, y, c, 1] = v_ref[c]
    barrier = pltpu.get_barrier_semaphore()
    for device in (up, down, sibling, plane_device(1, 0), plane_device(3, 0), plane_device(0, 1), plane_device(0, 3)):
        pl.semaphore_signal(barrier, inc=1, device_id=device, device_id_type=MESH)
    pl.semaphore_wait(barrier, 7)
    z_copy(0, 1, down).start()
    z_copy(0, 2, up).start()

    lane = lax.broadcasted_iota(jnp.int32, (R, 128), 1)
    for c in range(2):
        qv = q_ref[c] * jnp.asarray(0.125, BF)
        zero = jnp.zeros_like(qv)
        qm[c, :R] = jnp.where(lane < 64, qv, zero)
        qm[c, R:] = jnp.where(lane < 64, zero, qv)
    top[...] = jnp.full_like(top, NEG)
    acc[...] = jnp.zeros_like(acc)
    tot[...] = jnp.zeros_like(tot)

    def stage_first(k):
        @pl.when(k > 0)
        def _():
            send(piece(k, 0, 0), zs.at[k], zr.at[k], sibling).wait_recv()

            @pl.when((k % 2 == 1) & (k + 2 <= 7))
            def _():
                z_copy(k, k + 2, down).start()

            @pl.when((k % 2 == 0) & (k + 2 <= 6))
            def _():
                z_copy(k, k + 2, up).start()

        one_copy(k, 0).start()
        one_copy(k, 1).start()

    def stage_first_on(k):
        one_wait(k, 0)
        one_wait(k, 1)
        one_copy(k, 2).start()

    def stage_second(k):
        one_wait(k, 2)
        for m in range(4):
            two_copy(k, m, 0).start()
            two_copy(k, m, 1).start()

    def stage_second_on(k, m):
        two_wait(k, m, 0)
        two_wait(k, m, 1)
        two_copy(k, m, 2).start()

    def stage_pair(k):
        for m in range(4):
            two_wait(k, m, 2)
        pair_copy(k, True).start()

    def stage_ready(k):
        pair_copy(k, False).wait_recv()

    def keys_of(zz, xx, c):
        return (
            kv[zz, xx, :, :, c, 0].reshape(CH, 128),
            kv[zz, xx, :, :, c, 1].reshape(CH, 128),
        )

    def tasks(specs):
        loaded = []
        for tid, st, cq, ck, zz, xx, mask in specs:
            loaded.append((*keys_of(zz, xx, ck), qm[cq], top[st], tot[st], acc[st]))
        out = []
        for spec, (kb, vb, qq, old, total, a) in zip(specs, loaded):
            s = nt(kb, qq)
            if spec[-1] is not None:
                s = jnp.where(jnp.concatenate([spec[-1]] * 2, axis=1), s, NEG)
            new = jnp.maximum(old, jnp.max(s, axis=0, keepdims=True))
            p = jnp.exp(s - new)
            shrink = jnp.exp(old - new)
            total = total * shrink + jnp.sum(p, axis=0, keepdims=True)
            p = p.astype(BF)
            out.append((p, new, total, a * shrink + tn(vb, p)))
        for (tid, st, *_), (p, new, total, a) in zip(specs, out):
            w[tid] = p
            top[st] = new
            tot[st] = total
            acc[st] = a
            tops[tid] = new

    mine = core * 8 + inner

    def forward(k, h):
        zz, xx = unit_z(k), (x + 1 + h) % 4
        tid = 2 * (4 * k + h)
        own = ((zz * 4 + xx) % 16) * 2 + core
        here = ((z * 4 + x) % 16) * 2 + core
        c = jnp.where(own > here, 1, 0)
        if h < 3:
            tasks([(tid, 2, 1, 0, zz, xx, None), (tid + 1, c, c, c, zz, xx, None)])
            return
        edge = (k == 0) | (k == 7)

        @pl.when(jnp.logical_not(edge))
        def _():
            tasks([(tid, 2, 1, 0, zz, xx, None), (tid + 1, c, c, c, zz, xx, None)])

        @pl.when(edge)
        def _():
            key = lax.broadcasted_iota(jnp.int32, (CH, R), 0)
            tok = lax.broadcasted_iota(jnp.int32, (CH, R), 1) // 4
            blk = (key // 256) * 8 + ((key // 64) % 4) * 2 + zz // 4
            diag = (blk == mine) & (key % 64 <= tok)
            tasks([(tid, 2, 1, 0, zz, xx, None)])
            tasks([(tid + 1, 0, 0, 0, zz, xx, (blk < mine) | diag)])
            tasks([(64 + k // 7, 1, 1, 1, zz, xx, (blk > mine) | diag)])

    def gated(fn, k, *args):
        @pl.when((k >= 0) & (k < 8))
        def _():
            fn(k, *args)

    def turn(g, carry):
        gated(stage_first, g)
        gated(stage_second, g - 1)
        gated(stage_ready, g - 3)
        gated(forward, g - 3, 0)
        gated(forward, g - 3, 1)
        gated(stage_pair, g - 2)
        gated(stage_first_on, g)
        gated(stage_second_on, g - 1, 0)
        gated(stage_second_on, g - 1, 1)
        gated(forward, g - 3, 2)
        gated(stage_second_on, g - 1, 2)
        gated(stage_second_on, g - 1, 3)
        gated(forward, g - 3, 3)
        return carry

    lax.fori_loop(0, 11, turn, 0)

    head = lax.broadcasted_iota(jnp.int32, (1, R), 1) % 4
    lam = jnp.where(
        head == 0, lam_ref[0], jnp.where(head == 1, lam_ref[1], jnp.where(head == 2, lam_ref[2], lam_ref[3]))
    )
    gain = jnp.transpose(jnp.broadcast_to(gain_ref[...] * OUT, (R, 128)))
    for c in range(2):
        a, m, total = acc[c], top[c], tot[c]
        if c == 1:
            m2 = top[2]
            mm = jnp.maximum(m, m2)
            e1, e2 = jnp.exp(m - mm), jnp.exp(m2 - mm)
            a = a * e1 + acc[2] * e2
            total = total * e1 + tot[2] * e2
            m = mm
        a = a / total
        outs = [a[:, :R], a[:, R:]]
        lse = m + jnp.log(total)
        top[c] = lse
        if c == 1:
            top[2] = lse
        differ = outs[0] - lam * outs[1]
        inv = lax.rsqrt(jnp.mean(differ * differ, axis=0, keepdims=True) + EPS)
        att_ref[c] = jnp.transpose(gain * differ * inv).astype(BF)
        scaled = jnp.transpose(og_ref[c].astype(F32)) * gain
        dd = inv * scaled - differ * (inv * inv * inv) * jnp.mean(scaled * differ, axis=0, keepdims=True)
        for j in range(2):
            dots[c, :, j * R:j * R + R] = jnp.sum(dd * outs[j], axis=0, keepdims=True)
        back[c] = jnp.transpose(dd).astype(BF)

    grads[...] = jnp.zeros_like(grads)

    def back_tasks(specs):
        loaded = []
        for tid, st, cq, ck, zz, xx in specs:
            loaded.append((*keys_of(zz, xx, ck), back[cq], dots[cq], w[tid], tops[tid], top[st], grads[st]))
        out = []
        for kb, vb, bk, d, p, tp, lse, g in loaded:
            t = nt(vb, bk)
            slope = p * (jnp.concatenate([t, t], axis=1) - d).astype(BF)
            both = jnp.concatenate([tn(kb[:, :64], slope[:, :R]), tn(kb[:, 64:], slope[:, R:])], axis=1)
            out.append(g + both * jnp.exp(tp - lse))
        for spec, g in zip(specs, out):
            grads[spec[1]] = g

    def backward(n, carry):
        k, h = n // 4, n % 4
        zz, xx = unit_z(k), (x + 1 + h) % 4
        c = jnp.where((zz * 4 + xx) % 16 > (z * 4 + x) % 16, 1, 0)
        back_tasks([(2 * n, 2, 1, 0, zz, xx), (2 * n + 1, c, c, c, zz, xx)])
        return carry

    lax.fori_loop(0, 32, backward, 0)
    back_tasks([(64, 1, 1, 1, z, x)])
    back_tasks([(65, 1, 1, 1, (z + 4) % 8, x)])
    for c in range(2):
        g1, g2 = grads[c, :, :R], grads[c, :, R:]
        if c == 1:
            g1, g2 = g1 + grads[2, :, :R], g2 + grads[2, :, R:]
        qg_ref[c] = (0.125 * jnp.transpose(jnp.concatenate([g1, -lam * g2], axis=0))).astype(BF)

    def drain(k, carry):
        @pl.when(k > 0)
        def _():
            send(piece(k, 0, 0), zs.at[k], zr.at[k], sibling).wait_send()

        for slot in range(3):
            one_copy(k, slot).wait_send()
            for m in range(4):
                two_copy(k, m, slot).wait_send()
        pair_copy(k, True).wait_send()
        return carry

    lax.fori_loop(0, 8, drain, 0)


def body(queries, key_maps, values, lambdas, norm_gain, out_grad):
    V = pl.BlockSpec(memory_space=pltpu.VMEM)
    S = pl.BlockSpec(memory_space=pltpu.SMEM)
    dma = pltpu.SemaphoreType.DMA
    att, qg = pl.pallas_call(
        kernel,
        out_shape=(jax.ShapeDtypeStruct((2, R, 128), BF),) * 2,
        in_specs=[V, V, V, S, V, V],
        out_specs=(V, V),
        scratch_shapes=[
            pltpu.VMEM((8, 4, 2, 4, 2, 2, 64, 128), BF),
            pltpu.VMEM((66, CH, 2 * R), BF),
            pltpu.VMEM((2, 2 * R, 128), BF),
            pltpu.VMEM((3, 1, 2 * R), F32),
            pltpu.VMEM((3, 1, 2 * R), F32),
            pltpu.VMEM((3, 128, 2 * R), F32),
            pltpu.VMEM((66, 1, 2 * R), F32),
            pltpu.VMEM((2, R, 128), BF),
            pltpu.VMEM((2, 1, 2 * R), F32),
            pltpu.VMEM((3, 64, 2 * R), F32),
            dma((8,)), dma((8,)),
            dma((8, 3)), dma((8, 3)),
            dma((8, 4, 3)), dma((8, 4, 3)),
            dma((8,)), dma((8,)),
        ],
        compiler_params=pltpu.CompilerParams(
            collective_id=0, has_side_effects=True, vmem_limit_bytes=60 * 2**20
        ),
        cost_estimate=pl.CostEstimate(flops=13 * 10**9, bytes_accessed=2**21, transcendentals=17 * 10**6),
    )(
        queries.reshape(2, R, 128),
        key_maps.reshape(2, 64, 128),
        values.reshape(2, 64, 128),
        lambdas,
        norm_gain.reshape(1, 128),
        out_grad.reshape(2, R, 128),
    )
    shape = queries.shape
    return att.reshape(shape), qg.reshape(shape)


def solution(mesh):
    wide = P(None, "outer", "inner", None, None, None)
    keys = P(None, "outer", "inner", None, None)
    return jax.shard_map(
        body, mesh=mesh, in_specs=(wide, keys, keys, P(), P(), wide), out_specs=(wide, wide), check_vma=False
    )
```

time: 599 us -> 120 us (0.20); the launches traced: 593 us -> 120 us
  matrix products: 345 us -> 0 us
  Pallas kernels: 0 us -> 117 us
  waiting for transfers between devices: 97.9 us -> 0 us
  blocking collectives: 85.5 us -> 0 us
  other arithmetic: 22.3 us -> 0 us
  local copies, waits for them, and re-layouts: 22.3 us -> 2.3 us
  between operations: 14.5 us -> 0.65 us
    dot_general x231 -> x0, matrix products: 345 us -> none  [the longest x99 128 us: contract(): lax.dot_general(left_op, right_op, (((1,), (1,)), ((), ())), preferred_el...]
    pallas_call x0 -> x1, Pallas kernels: none -> 117 us  [body(): pl.pallas_call(kernel, out_shape=(jax.ShapeDtypeStruct((2, R, 128), BF),)...]
    all_gather x2 -> x0, waiting for transfers between devices: 97.9 us -> none  [the longest x1 63.2 us: body(): lax.all_gather(near_values, 'outer', axis=1, tiled=True)]
    all_gather x2 -> x0, blocking collectives: 85.5 us -> none  [the longest x1 43.7 us: body(): lax.all_gather(key_maps, 'inner', axis=2, tiled=True)]
    reduce_sum x36 -> x0, other arithmetic: 16.1 us -> none  [the longest x33 15 us: absorb(): run_sum = run_sum * shrink + jnp.sum(weights, axis=1)]
    slice x3 -> x0, local copies, waits for them, and re-layouts: 15.6 us -> none  [the longest x1 7.32 us: split_segments(): upper_keys = key_whole[1].reshape(span_len, key_whole.shape[4])]
  transfers between devices with their start and end apart: 2 -> 0, of which waited for: 2 -> 0; matrix products, arithmetic and copies ran while one was open for 2% -> 0% of each run, Pallas kernels for 0% -> 0%
where the time goes in v1:
time: 120 us
  Pallas kernels  117 us (98%)
  local copies, waits for them, and re-layouts  2.3 us (2%)
    pallas_call x1, Pallas kernels, body(): pl.pallas_call(kernel, out_shape=(jax.ShapeDtypeStruct((2, R, 128), BF),)...  117 us

profile of v1, /device:TPU:1, one launch (start us, length us, event | category | flops | bytes accessed | tf_op | source)
XLA Modules:
  0.0 119.7 jit_solution(6574634195678320430)
XLA Ops:
  0.6 116.8 %shard_map.77 = (bf16[2,256,128]{2,1,0:T(8,128)(2,1)}, bf16[2,256,128]{2,1,0:T(8,128)(2,1)}) custom-call(bf16[2,256,128]{2,1,0:T(8,128)(2,1)} %bitcast.13, bf16[2,64,128]{2,1,0:T(8,128)(2,1)} %bitcast.15, bf16[2,64,128]{2,1,0:T(8,128)(2,1)} %bitcast.16, f32[4]{0:T(128)} %lam_ref.1, f32[1,128]{1,0:T(1,128)} %bitcast.17, bf16[2,256,128]{2,1,0:T(8,128)(2,1)} %bitcast.14), custom_call_target="tpu_custom_call" | custom-call | flops 12999999488 | bytes 2097152 | tf_op jit(solution)/shard_map/pallas_call | solution.py:311
  117.4 0.0 copy-start
  117.4 1.6 %copy.12 = bf16[2,1,1,64,4,128]{5,4,3,2,1,0:T(4,128)(2,1)} copy(bf16[2,1,1,64,4,128]{5,4,3,2,1,0:T(4,128)(2,1)} %bitcast.12) | data formatting | bytes 262144
  119.1 0.0 copy-done
  119.1 0.7 copy.13
Async XLA Ops:
  117.4 1.7 %copy-start = (bf16[2,256,128]{2,1,0:T(8,128)(2,1)S(1)}, bf16[2,256,128]{2,1,0:T(8,128)(2,1)}, u32[]{:S(2)}) copy-start(bf16[2,256,128]{2,1,0:T(8,128)(2,1)} %get-tuple-element.5) | copy-start | bytes 393220

commit v2 on v1

v2 whole, which is shorter than its diff:
```python
import math

import jax
import jax.numpy as jnp
from jax import lax
from jax.experimental import pallas as pl
from jax.experimental.pallas import tpu as pltpu
from jax.sharding import PartitionSpec as P

lam_init = 0.8 - 0.6 * math.exp(-3.3)
OUT = 1.0 - lam_init
EPS = 1e-5
NEG = -1e30
F32, BF = jnp.float32, jnp.bfloat16
R = 256
CH = 512
MESH = pl.DeviceIdType.MESH
ORDER = ((3, 0), (6, 1), (8, 2), (10, 3), (11, 6), (12, 4), (13, 7), (14, 5))
LINES = (9, 12)


def nt(a, b):
    return lax.dot_general(a, b, (((1,), (1,)), ((), ())), preferred_element_type=F32)


def tn(a, b):
    return lax.dot_general(a, b, (((0,), (0,)), ((), ())), preferred_element_type=F32)


def device_at(x, y, z, core):
    return (y * 2 + z // 4, ((z % 4) * 4 + x) * 2 + core)


def kernel(
    q_ref, k_ref, v_ref, lam_ref, gain_ref, og_ref, att_ref, qg_ref,
    kv, w, qm, top, tot, acc, tops, back, dots, grads, sbuf, bounds,
    sent, zr, pr, r1, r2, sr,
):
    inner, outer = lax.axis_index("inner"), lax.axis_index("outer")
    y, z = inner // 2, (inner % 2) * 4 + outer // 8
    x, core = (outer // 2) % 4, outer % 2
    first = core == 0
    a_pos, b_pos = jnp.where(first, x, y), jnp.where(first, y, x)

    def place(a, b):
        return jnp.where(first, a, b), jnp.where(first, b, a)

    def plane_device(da, db):
        px, py = place((a_pos + da) % 4, (b_pos + db) % 4)
        return device_at(px, py, z, core)

    sibling = device_at(x, y, z, 1 - core)
    SIDE = (0, 3, 1, 2)

    def unit_step(k):
        half = jnp.where(k >= 6, 1, jnp.where(k == 0, 0, (k + 1) // 2 + 1))
        ahead = jnp.where(k >= 6, k == 6, k % 2 == 1)
        return jnp.where(ahead, half, 8 - half)

    def unit_z(k):
        return (z + unit_step(k)) % 8

    def piece(k, da, db):
        px, py = place((a_pos + da) % 4, (b_pos + db) % 4)
        return kv.at[unit_z(k), px, core, py]

    def send(ref, send_sem, recv_sem, device):
        return pltpu.make_async_remote_copy(
            src_ref=ref, dst_ref=ref, send_sem=send_sem, recv_sem=recv_sem,
            device_id=device, device_id_type=MESH,
        )

    def z_copy(k):
        ref = kv.at[z, x, core, y]
        return send(ref, sent.at[k], zr.at[k], device_at(x, y, (z + 8 - unit_step(k)) % 8, core))

    def line_do(i, k, n, act):
        b = (b_pos + SIDE[n]) % 4
        device = device_at(x, y, (z + (7, 1)[i]) % 8, core)

        @pl.when(first)
        def _():
            act(send(kv.at[unit_z(k), :, core, b], sent.at[7], pr.at[i, n], device))

        @pl.when(jnp.logical_not(first))
        def _():
            act(send(kv.at[unit_z(k), b, core], sent.at[7], pr.at[i, n], device))

    def line_send(n):
        for i in range(2):
            line_do(i, 0, n, lambda c: c.start())

    def z_wait(k):
        send(piece(k, 0, 0), sent.at[k], zr.at[k], sibling).wait_recv()

    def one_sent(k):
        return sent.at[jnp.where(k == 0, 6, k)]

    def one_copy(k, slot):
        sign = 1 - 2 * (k % 2)
        if slot == 2:
            return send(piece(k, 4 - sign, 0), one_sent(k), r1.at[k, 2], plane_device(4 + sign, 0))
        return send(piece(k, 0, 0), one_sent(k), r1.at[k, slot], plane_device((1, 3)[slot], 0))

    def one_wait(k, slot):
        send(piece(k, (3, 1, 2)[slot], 0), one_sent(k), r1.at[k, slot], sibling).wait_recv()

    def two_copy(k, m, slot):
        if slot == 2:
            sign = (1, 3)[m % 2]
            return send(piece(k, SIDE[m], 4 - sign), sent.at[k], r2.at[k, m, 2], plane_device(0, sign))
        return send(piece(k, SIDE[m], 0), sent.at[k], r2.at[k, m, slot], plane_device(0, (1, 3)[slot]))

    def two_wait(k, m, slot):
        send(piece(k, SIDE[m], (3, 1, 2)[slot]), sent.at[k], r2.at[k, m, slot], sibling).wait_recv()

    def pair_copy(k, mine):
        ref = kv.at[unit_z(k), :, core if mine else 1 - core]
        return send(ref, sent.at[8], sr.at[k], sibling)

    for c in range(2):
        kv[z, x, core, y, c, 0] = k_ref[c]
        kv[z, x, core, y, c, 1] = v_ref[c]
    barrier = pltpu.get_barrier_semaphore()
    partners = [sibling, plane_device(1, 0), plane_device(3, 0), plane_device(0, 1), plane_device(0, 3)]
    partners += [device_at(x, y, (z + d) % 8, core) for d in range(1, 8)]
    for device in partners:
        pl.semaphore_signal(barrier, inc=1, device_id=device, device_id_type=MESH)
    lane = lax.broadcasted_iota(jnp.int32, (R, 128), 1)
    for c in range(2):
        qv = q_ref[c] * jnp.asarray(0.125, BF)
        zero = jnp.zeros_like(qv)
        qm[c, :R] = jnp.where(lane < 64, qv, zero)
        qm[c, R:] = jnp.where(lane < 64, zero, qv)
    top[...] = jnp.full_like(top, NEG)
    acc[...] = jnp.zeros_like(acc)
    tot[...] = jnp.zeros_like(tot)

    pl.semaphore_wait(barrier, len(partners))

    def first_send(k):
        one_copy(k, 0).start()
        one_copy(k, 1).start()

    def first_send_after(k):
        z_wait(k)
        first_send(k)

    def first_pass(k):
        one_wait(k, 0)
        one_wait(k, 1)
        one_copy(k, 2).start()

    def second_send(k, m):
        two_copy(k, m, 0).start()
        two_copy(k, m, 1).start()

    def second_sends(k):
        for m in range(3):
            second_send(k, m)
        one_wait(k, 2)
        second_send(k, 3)

    def second_pass(k, m):
        two_wait(k, m, 0)
        two_wait(k, m, 1)
        two_copy(k, m, 2).start()

    def pair_send(k):
        for m in range(4):
            two_wait(k, m, 2)
        pair_copy(k, True).start()

    def pair_send_after(i):
        for n in range(4):
            line_do(i, 6 + i, n, lambda c: c.wait_recv())
        pair_copy(6 + i, True).start()

    def ready(k):
        pair_copy(k, False).wait_recv()

    def keys_of(zz, xx, c):
        return (
            kv[zz, xx, :, :, c, 0].reshape(CH, 128),
            kv[zz, xx, :, :, c, 1].reshape(CH, 128),
        )

    mine = core * 8 + inner

    def step_of(k, h):
        zz, xx = unit_z(k), (x + 1 + h) % 4
        c = jnp.where((zz * 4 + xx) % 16 > (z * 4 + x) % 16, 1, 0)
        n = 4 * k + h
        return zz, xx, ((2 * n, 2, 1, 0), (2 * n + 1, c, c, c))

    def edge_masks(zz):
        key = lax.broadcasted_iota(jnp.int32, (CH, 2 * R), 0)
        tok = (lax.broadcasted_iota(jnp.int32, (CH, 2 * R), 1) % R) // 4
        blk = (key // 256) * 8 + ((key // 64) % 4) * 2 + zz // 4
        diag = (blk == mine) & (key % 64 <= tok)
        return (blk < mine) | diag, (blk > mine) | diag

    def forward(k, nxt, cur):
        if nxt is not None:
            par = nxt % 2
            zz, xx, parts = step_of(k, nxt)
            heads = [(keys_of(zz, xx, ck)[0], qm[cq], top[st]) for _, st, cq, ck in parts]
        if cur is not None:
            was = cur % 2
            zc, xc, done = step_of(k, cur)
            tails = [(keys_of(zc, xc, ck)[1], bounds[was, i, 0], bounds[was, i, 1], tot[st], acc[st])
                     for i, (_, st, cq, ck) in enumerate(done)]
        new_tops, sums = [], []
        for i in range(2):
            if nxt is not None:
                kb, qq, old = heads[i]
                s = nt(kb, qq)
                if nxt == 3 and i == 1:
                    off_edge = (zz % 4 != z % 4) | (xx != x)
                    s = jnp.where(edge_masks(zz)[0] | off_edge, s, NEG)
                sbuf[par, i] = s
                new_tops.append((old, jnp.maximum(old, jnp.max(s, axis=0, keepdims=True))))
            if cur is not None:
                vb, old, new, total, a = tails[i]
                p = jnp.exp(sbuf[was, i] - new)
                shrink = jnp.exp(old - new)
                total = total * shrink + jnp.sum(p, axis=0, keepdims=True)
                p = p.astype(BF)
                w[done[i][0]] = p
                sums.append((total, a * shrink + tn(vb, p)))
        if nxt is not None:
            for i, (old, new) in enumerate(new_tops):
                bounds[par, i, 0] = old
                bounds[par, i, 1] = new
                top[parts[i][1]] = new
                tops[parts[i][0]] = new
        if cur is not None:
            for i, (total, a) in enumerate(sums):
                tot[done[i][1]] = total
                acc[done[i][1]] = a

    def forward_edge(k):
        @pl.when((k == 0) | (k == 5))
        def _():
            zz = unit_z(k)
            kb, vb = keys_of(zz, x, 1)
            s = jnp.where(edge_masks(zz)[1], nt(kb, qm[1]), NEG)
            old = top[1]
            new = jnp.maximum(old, jnp.max(s, axis=0, keepdims=True))
            p = jnp.exp(s - new)
            shrink = jnp.exp(old - new)
            tot[1] = tot[1] * shrink + jnp.sum(p, axis=0, keepdims=True)
            p = p.astype(BF)
            acc[1] = acc[1] * shrink + tn(vb, p)
            top[1] = new
            w[64 + k // 5] = p
            tops[64 + k // 5] = new

    def gated(fn, k, last, *args):
        @pl.when(k <= last)
        def _():
            fn(k, *args)

    z_copy(1).start()
    z_copy(2).start()
    first_send(0)
    first_pass(0)
    z_copy(3).start()
    z_copy(4).start()
    for m in range(3):
        second_send(0, m)
    first_send_after(1)
    first_send_after(2)
    z_copy(5).start()
    one_wait(0, 2)
    second_send(0, 3)
    line_send(0)
    for m in range(4):
        second_pass(0, m)
    line_send(1)
    line_send(2)
    first_pass(1)
    first_pass(2)
    second_sends(1)
    first_send_after(3)
    pair_send(0)
    line_send(3)

    def half_turn(t, carry):
        g, late = t // 2, t % 2 == 1

        @pl.when(jnp.logical_not(late))
        def _():
            @pl.when(g <= 4)
            def _():
                for m in range(3):
                    second_send(g + 1, m)

            @pl.when(g <= 2)
            def _():
                first_send_after(g + 3)

        @pl.when(late)
        def _():
            @pl.when(g <= 4)
            def _():
                one_wait(g + 1, 2)
                second_send(g + 1, 3)

            @pl.when((g >= 2) & (g <= 6))
            def _():
                pair_send(g - 1)

            @pl.when(g <= 5)
            def _():
                for m in range(4):
                    second_pass(g, m)

            @pl.when(g <= 3)
            def _():
                first_pass(g + 2)

        unit = jnp.int32(-1)
        for when, what in ORDER:
            unit = jnp.where(t == when, what, unit)

        @pl.when(unit >= 0)
        def _():
            ready(unit)
            forward(unit, 0, None)
            forward(unit, 1, 0)
            forward(unit, 2, 1)
            forward(unit, 3, 2)
            forward(unit, None, 3)
            forward_edge(unit)

        for i in range(2):

            @pl.when(t == LINES[i])
            def _():
                pair_send_after(i)

        return carry

    lax.fori_loop(2, 15, half_turn, 0)

    head = lax.broadcasted_iota(jnp.int32, (1, R), 1) % 4
    lam = jnp.where(
        head == 0, lam_ref[0], jnp.where(head == 1, lam_ref[1], jnp.where(head == 2, lam_ref[2], lam_ref[3]))
    )
    gain = jnp.transpose(jnp.broadcast_to(gain_ref[...] * OUT, (R, 128)))
    for c in range(2):
        a, m, total = acc[c], top[c], tot[c]
        if c == 1:
            m2 = top[2]
            mm = jnp.maximum(m, m2)
            e1, e2 = jnp.exp(m - mm), jnp.exp(m2 - mm)
            a = a * e1 + acc[2] * e2
            total = total * e1 + tot[2] * e2
            m = mm
        a = a / total
        outs = [a[:, :R], a[:, R:]]
        lse = m + jnp.log(total)
        top[c] = lse
        if c == 1:
            top[2] = lse
        differ = outs[0] - lam * outs[1]
        inv = lax.rsqrt(jnp.mean(differ * differ, axis=0, keepdims=True) + EPS)
        att_ref[c] = jnp.transpose(gain * differ * inv).astype(BF)
        scaled = jnp.transpose(og_ref[c].astype(F32)) * gain
        dd = inv * scaled - differ * (inv * inv * inv) * jnp.mean(scaled * differ, axis=0, keepdims=True)
        for j in range(2):
            dots[c, :, j * R:j * R + R] = jnp.sum(dd * outs[j], axis=0, keepdims=True)
        back[c] = jnp.transpose(dd).astype(BF)

    grads[...] = jnp.zeros_like(grads)

    def slopes(t, d, p):
        return [(t - d[:, j * R:j * R + R]).astype(BF) * p[:, j * R:j * R + R] for j in range(2)]

    def gradient(kb, pair):
        return jnp.concatenate([tn(kb, pair[0])[:64], tn(kb, pair[1])[64:]], axis=1)

    def backward(nxt, cur, par):
        if nxt is not None:
            zz, xx, parts = step_of(nxt // 4, nxt % 4)
            heads = [(keys_of(zz, xx, ck)[1], back[cq]) for _, _, cq, ck in parts]
        if cur is not None:
            zc, xc, done = step_of(cur // 4, cur % 4)
            tails = [(keys_of(zc, xc, ck)[0], dots[cq], tops[tid], top[st], grads[st]) for tid, st, cq, ck in done]
        sums = []
        for i in range(2):
            if nxt is not None:
                vb, bk = heads[i]
                sbuf[par, i, :, :R] = nt(vb, bk)
            if cur is not None:
                kb, d, bound, lse, g = tails[i]
                pair = slopes(sbuf[1 - par, i, :, :R], d, w[done[i][0]])
                sums.append(g + gradient(kb, pair) * jnp.exp(bound - lse))
        if cur is not None:
            for i, g in enumerate(sums):
                grads[done[i][1]] = g

    def two_steps(n, carry):
        backward(2 * n + 1, 2 * n, 1)
        backward(2 * n + 2, 2 * n + 1, 0)
        return carry

    backward(0, None, 0)
    lax.fori_loop(0, 15, two_steps, 0)
    backward(31, 30, 1)
    backward(None, 31, 0)
    for i, zz in enumerate((z, (z + 4) % 8)):
        kb, vb = keys_of(zz, x, 1)
        pair = slopes(nt(vb, back[1]), dots[1], w[64 + i])
        grads[1] = grads[1] + gradient(kb, pair) * jnp.exp(tops[64 + i] - top[1])
    for c in range(2):
        g1, g2 = grads[c, :, :R], grads[c, :, R:]
        if c == 1:
            g1, g2 = g1 + grads[2, :, :R], g2 + grads[2, :, R:]
        qg_ref[c] = (0.125 * jnp.transpose(jnp.concatenate([g1, -lam * g2], axis=0))).astype(BF)

    def drain(ref, k):
        send(ref, sent.at[k], sent.at[k], sibling).wait_send()

    drain(kv.at[0, 0:3, 0], 0)
    for k in range(1, 6):
        drain(kv.at[0, :, 0], k)
    drain(kv.at[0, 0, 0, 0:3], 6)
    drain(kv.at[0], 7)
    drain(kv.at[0:4], 8)


def body(queries, key_maps, values, lambdas, norm_gain, out_grad):
    V = pl.BlockSpec(memory_space=pltpu.VMEM)
    S = pl.BlockSpec(memory_space=pltpu.SMEM)
    dma = pltpu.SemaphoreType.DMA
    att, qg = pl.pallas_call(
        kernel,
        out_shape=(jax.ShapeDtypeStruct((2, R, 128), BF),) * 2,
        in_specs=[V, V, V, S, V, V],
        out_specs=(V, V),
        scratch_shapes=[
            pltpu.VMEM((8, 4, 2, 4, 2, 2, 64, 128), BF),
            pltpu.VMEM((66, CH, 2 * R), BF),
            pltpu.VMEM((2, 2 * R, 128), BF),
            pltpu.VMEM((3, 1, 2 * R), F32),
            pltpu.VMEM((3, 1, 2 * R), F32),
            pltpu.VMEM((3, 128, 2 * R), F32),
            pltpu.VMEM((66, 1, 2 * R), F32),
            pltpu.VMEM((2, R, 128), BF),
            pltpu.VMEM((2, 1, 2 * R), F32),
            pltpu.VMEM((3, 64, 2 * R), F32),
            pltpu.VMEM((2, 2, CH, 2 * R), F32),
            pltpu.VMEM((2, 2, 2, 1, 2 * R), F32),
            dma((9,)), dma((8,)), dma((2, 4)), dma((6, 3)), dma((6, 4, 3)), dma((8,)),
        ],
        compiler_params=pltpu.CompilerParams(
            collective_id=0, has_side_effects=True, vmem_limit_bytes=62 * 2**20
        ),
        cost_estimate=pl.CostEstimate(flops=13 * 10**9, bytes_accessed=2**21, transcendentals=17 * 10**6),
    )(
        queries.reshape(2, R, 128),
        key_maps.reshape(2, 64, 128),
        values.reshape(2, 64, 128),
        lambdas,
        norm_gain.reshape(1, 128),
        out_grad.reshape(2, R, 128),
    )
    shape = queries.shape
    return att.reshape(shape), qg.reshape(shape)


def solution(mesh):
    wide = P(None, "outer", "inner", None, None, None)
    keys = P(None, "outer", "inner", None, None)
    return jax.shard_map(
        body, mesh=mesh, in_specs=(wide, keys, keys, P(), P(), wide), out_specs=(wide, wide), check_vma=False
    )
```

time: 120 us -> 86.4 us (0.72)
  Pallas kernels: 117 us -> 83.3 us
    pallas_call x1, Pallas kernels: 117 us -> 83.3 us  [body(): pl.pallas_call(kernel, out_shape=(jax.ShapeDtypeStruct((2, R, 128), BF),)...]
where the time goes in v2:
time: 86.4 us; the launch traced here: 86.3 us
  Pallas kernels  83.3 us (96%)
  local copies, waits for them, and re-layouts  2.3 us (3%)
    pallas_call x1, Pallas kernels, body(): pl.pallas_call(kernel, out_shape=(jax.ShapeDtypeStruct((2, R, 128), BF),)...  83.3 us
    unnamed x4, local copies, waits for them, and re-layouts  2.3 us

profile of v2, /device:TPU:1, one launch (start us, length us, event | category | flops | bytes accessed | tf_op | source)
XLA Modules:
  0.0 86.3 jit_solution(17814275421869152017)
XLA Ops:
  0.6 83.3 %shard_map.77 = (bf16[2,256,128]{2,1,0:T(8,128)(2,1)}, bf16[2,256,128]{2,1,0:T(8,128)(2,1)}) custom-call(bf16[2,256,128]{2,1,0:T(8,128)(2,1)} %bitcast.13, bf16[2,64,128]{2,1,0:T(8,128)(2,1)} %bitcast.15, bf16[2,64,128]{2,1,0:T(8,128)(2,1)} %bitcast.16, f32[4]{0:T(128)} %lam_ref.1, f32[1,128]{1,0:T(1,128)} %bitcast.17, bf16[2,256,128]{2,1,0:T(8,128)(2,1)} %bitcast.14), custom_call_target="tpu_custom_call" | custom-call | flops 12999999488 | bytes 2097152 | tf_op jit(solution)/shard_map/pallas_call | solution.py:438
  84.0 0.0 copy-start
  84.0 1.6 %copy.12 = bf16[2,1,1,64,4,128]{5,4,3,2,1,0:T(4,128)(2,1)} copy(bf16[2,1,1,64,4,128]{5,4,3,2,1,0:T(4,128)(2,1)} %bitcast.12) | data formatting | bytes 262144
  85.6 0.0 copy-done
  85.6 0.7 copy.13
Async XLA Ops:
  84.0 1.7 %copy-start = (bf16[2,256,128]{2,1,0:T(8,128)(2,1)S(1)}, bf16[2,256,128]{2,1,0:T(8,128)(2,1)}, u32[]{:S(2)}) copy-start(bf16[2,256,128]{2,1,0:T(8,128)(2,1)} %get-tuple-element.5) | copy-start | bytes 393220

commit v3 on v2

--- a/solution.py
+++ b/solution.py
@@ -15,7 +15,7 @@
 R = 256
 CH = 512
 MESH = pl.DeviceIdType.MESH
-ORDER = ((3, 0), (6, 1), (8, 2), (10, 3), (11, 6), (12, 4), (13, 7), (14, 5))
+ORDER = ((4, 0), (6, 1), (8, 2), (10, 3), (11, 6), (12, 4), (14, 7), (15, 5))
 LINES = (9, 12)
 
 
@@ -53,8 +53,8 @@
     SIDE = (0, 3, 1, 2)
 
     def unit_step(k):
-        half = jnp.where(k >= 6, 1, jnp.where(k == 0, 0, (k + 1) // 2 + 1))
-        ahead = jnp.where(k >= 6, k == 6, k % 2 == 1)
+        half = jnp.where(k >= 6, 1, jnp.where(k >= 4, 3, jnp.where(k == 3, 4, jnp.where(k == 0, 0, 2))))
+        ahead = (k == 1) | (k == 4) | (k == 6)
         return jnp.where(ahead, half, 8 - half)
 
     def unit_z(k):
@@ -240,7 +240,7 @@
                 acc[done[i][1]] = a
 
     def forward_edge(k):
-        @pl.when((k == 0) | (k == 5))
+        @pl.when((k == 0) | (k == 3))
         def _():
             zz = unit_z(k)
             kb, vb = keys_of(zz, x, 1)
@@ -253,8 +253,8 @@
             p = p.astype(BF)
             acc[1] = acc[1] * shrink + tn(vb, p)
             top[1] = new
-            w[64 + k // 5] = p
-            tops[64 + k // 5] = new
+            w[64 + k // 3] = p
+            tops[64 + k // 3] = new
 
     def gated(fn, k, last, *args):
         @pl.when(k <= last)
@@ -307,10 +307,6 @@
                 one_wait(g + 1, 2)
                 second_send(g + 1, 3)
 
-            @pl.when((g >= 2) & (g <= 6))
-            def _():
-                pair_send(g - 1)
-
             @pl.when(g <= 5)
             def _():
                 for m in range(4):
@@ -319,6 +315,10 @@
             @pl.when(g <= 3)
             def _():
                 first_pass(g + 2)
+
+            @pl.when((g >= 2) & (g <= 6))
+            def _():
+                pair_send(g - 1)
 
         unit = jnp.int32(-1)
         for when, what in ORDER:
@@ -342,7 +342,7 @@
 
         return carry
 
-    lax.fori_loop(2, 15, half_turn, 0)
+    lax.fori_loop(2, 16, half_turn, 0)
 
     head = lax.broadcasted_iota(jnp.int32, (1, R), 1) % 4
     lam = jnp.where(
@@ -401,14 +401,15 @@
             for i, g in enumerate(sums):
                 grads[done[i][1]] = g
 
-    def two_steps(n, carry):
-        backward(2 * n + 1, 2 * n, 1)
-        backward(2 * n + 2, 2 * n + 1, 0)
+    def four_steps(n, carry):
+        for i in range(4):
+            backward(4 * n + i + 1, 4 * n + i, (i + 1) % 2)
         return carry
 
     backward(0, None, 0)
-    lax.fori_loop(0, 15, two_steps, 0)
-    backward(31, 30, 1)
+    lax.fori_loop(0, 7, four_steps, 0)
+    for n in range(28, 31):
+        backward(n + 1, n, (n + 1) % 2)
     backward(None, 31, 0)
     for i, zz in enumerate((z, (z + 4) % 8)):
         kb, vb = keys_of(zz, x, 1)

time: 86.4 us -> 84.1 us (0.973)
  Pallas kernels: 83.3 us -> 81.1 us
    pallas_call x1, Pallas kernels: 83.3 us -> 81.1 us  [body(): pl.pallas_call(kernel, out_shape=(jax.ShapeDtypeStruct((2, R, 128), BF),)...]
where the time goes in v3:
time: 84.1 us; the launch traced here: 84 us
  Pallas kernels  81.1 us (96%)
  local copies, waits for them, and re-layouts  2.3 us (3%)
    pallas_call x1, Pallas kernels, body(): pl.pallas_call(kernel, out_shape=(jax.ShapeDtypeStruct((2, R, 128), BF),)...  81.1 us
    unnamed x4, local copies, waits for them, and re-layouts  2.3 us

profile of v3, /device:TPU:1, one launch (start us, length us, event | category | flops | bytes accessed | tf_op | source)
XLA Modules:
  0.0 84.0 jit_solution(7641501245640767383)
XLA Ops:
  0.6 81.1 %shard_map.77 = (bf16[2,256,128]{2,1,0:T(8,128)(2,1)}, bf16[2,256,128]{2,1,0:T(8,128)(2,1)}) custom-call(bf16[2,256,128]{2,1,0:T(8,128)(2,1)} %bitcast.13, bf16[2,64,128]{2,1,0:T(8,128)(2,1)} %bitcast.15, bf16[2,64,128]{2,1,0:T(8,128)(2,1)} %bitcast.16, f32[4]{0:T(128)} %lam_ref.1, f32[1,128]{1,0:T(1,128)} %bitcast.17, bf16[2,256,128]{2,1,0:T(8,128)(2,1)} %bitcast.14), custom_call_target="tpu_custom_call" | custom-call | flops 12999999488 | bytes 2097152 | tf_op jit(solution)/shard_map/pallas_call | solution.py:439
  81.7 0.0 copy-start
  81.7 1.6 %copy.12 = bf16[2,1,1,64,4,128]{5,4,3,2,1,0:T(4,128)(2,1)} copy(bf16[2,1,1,64,4,128]{5,4,3,2,1,0:T(4,128)(2,1)} %bitcast.12) | data formatting | bytes 262144
  83.4 0.0 copy-done
  83.4 0.7 copy.13
Async XLA Ops:
  81.7 1.7 %copy-start = (bf16[2,256,128]{2,1,0:T(8,128)(2,1)S(1)}, bf16[2,256,128]{2,1,0:T(8,128)(2,1)}, u32[]{:S(2)}) copy-start(bf16[2,256,128]{2,1,0:T(8,128)(2,1)} %get-tuple-element.5) | copy-start | bytes 393220

commit v4 on v3

--- a/solution.py
+++ b/solution.py
@@ -401,20 +401,23 @@
             for i, g in enumerate(sums):
                 grads[done[i][1]] = g
 
-    def four_steps(n, carry):
-        for i in range(4):
-            backward(4 * n + i + 1, 4 * n + i, (i + 1) % 2)
+    def eight_steps(n, carry):
+        for i in range(8):
+            backward(8 * n + i + 1, 8 * n + i, (i + 1) % 2)
         return carry
 
     backward(0, None, 0)
-    lax.fori_loop(0, 7, four_steps, 0)
-    for n in range(28, 31):
+    lax.fori_loop(0, 3, eight_steps, 0)
+    for n in range(24, 31):
         backward(n + 1, n, (n + 1) % 2)
+    extra = [keys_of(zz, x, 1) for zz in (z, (z + 4) % 8)]
+    through = [nt(vb, back[1]) for _, vb in extra]
     backward(None, 31, 0)
-    for i, zz in enumerate((z, (z + 4) % 8)):
-        kb, vb = keys_of(zz, x, 1)
-        pair = slopes(nt(vb, back[1]), dots[1], w[64 + i])
-        grads[1] = grads[1] + gradient(kb, pair) * jnp.exp(tops[64 + i] - top[1])
+    added = [
+        gradient(extra[i][0], slopes(through[i], dots[1], w[64 + i])) * jnp.exp(tops[64 + i] - top[1])
+        for i in range(2)
+    ]
+    grads[1] = grads[1] + added[0] + added[1]
     for c in range(2):
         g1, g2 = grads[c, :, :R], grads[c, :, R:]
         if c == 1:

time: 84.1 us -> 83.2 us (0.989)
  Pallas kernels: 81.1 us -> 80.2 us
    pallas_call x1, Pallas kernels: 81.1 us -> 80.2 us  [body(): pl.pallas_call(kernel, out_shape=(jax.ShapeDtypeStruct((2, R, 128), BF),)...]
where the time goes in v4:
time: 83.2 us; the launch traced here: 83.1 us
  Pallas kernels  80.2 us (96%)
  local copies, waits for them, and re-layouts  2.3 us (3%)
    pallas_call x1, Pallas kernels, body(): pl.pallas_call(kernel, out_shape=(jax.ShapeDtypeStruct((2, R, 128), BF),)...  80.2 us
    unnamed x4, local copies, waits for them, and re-layouts  2.3 us

profile of v4, /device:TPU:1, one launch (start us, length us, event | category | flops | bytes accessed | tf_op | source)
XLA Modules:
  0.0 83.1 jit_solution(15435440772117531444)
XLA Ops:
  0.6 80.2 %shard_map.77 = (bf16[2,256,128]{2,1,0:T(8,128)(2,1)}, bf16[2,256,128]{2,1,0:T(8,128)(2,1)}) custom-call(bf16[2,256,128]{2,1,0:T(8,128)(2,1)} %bitcast.13, bf16[2,64,128]{2,1,0:T(8,128)(2,1)} %bitcast.15, bf16[2,64,128]{2,1,0:T(8,128)(2,1)} %bitcast.16, f32[4]{0:T(128)} %lam_ref.1, f32[1,128]{1,0:T(1,128)} %bitcast.17, bf16[2,256,128]{2,1,0:T(8,128)(2,1)} %bitcast.14), custom_call_target="tpu_custom_call" | custom-call | flops 12999999488 | bytes 2097152 | tf_op jit(solution)/shard_map/pallas_call | solution.py:442
  80.8 0.0 copy-start
  80.8 1.6 %copy.12 = bf16[2,1,1,64,4,128]{5,4,3,2,1,0:T(4,128)(2,1)} copy(bf16[2,1,1,64,4,128]{5,4,3,2,1,0:T(4,128)(2,1)} %bitcast.12) | data formatting | bytes 262144
  82.5 0.0 copy-done
  82.5 0.7 copy.13
Async XLA Ops:
  80.8 1.7 %copy-start = (bf16[2,256,128]{2,1,0:T(8,128)(2,1)S(1)}, bf16[2,256,128]{2,1,0:T(8,128)(2,1)}, u32[]{:S(2)}) copy-start(bf16[2,256,128]{2,1,0:T(8,128)(2,1)} %get-tuple-element.5) | copy-start | bytes 393220

commit v5 on v4

--- a/solution.py
+++ b/solution.py
@@ -193,12 +193,14 @@
         n = 4 * k + h
         return zz, xx, ((2 * n, 2, 1, 0), (2 * n + 1, c, c, c))
 
-    def edge_masks(zz):
-        key = lax.broadcasted_iota(jnp.int32, (CH, 2 * R), 0)
-        tok = (lax.broadcasted_iota(jnp.int32, (CH, 2 * R), 1) % R) // 4
+    def edge_masks(zz, all_seen):
+        key = lax.broadcasted_iota(jnp.int32, (CH, 1), 0)
+        tok = (lax.broadcasted_iota(jnp.int32, (1, 2 * R), 1) % R) // 4
         blk = (key // 256) * 8 + ((key // 64) % 4) * 2 + zz // 4
-        diag = (blk == mine) & (key % 64 <= tok)
-        return (blk < mine) | diag, (blk > mine) | diag
+        own = jnp.where(blk == mine, key % 64, 64)
+        low = jnp.where((blk < mine) | all_seen, -1, own)
+        high = jnp.where(blk > mine, -1, own)
+        return low <= tok, high <= tok
 
     def forward(k, nxt, cur):
         if nxt is not None:
@@ -217,7 +219,7 @@
                 s = nt(kb, qq)
                 if nxt == 3 and i == 1:
                     off_edge = (zz % 4 != z % 4) | (xx != x)
-                    s = jnp.where(edge_masks(zz)[0] | off_edge, s, NEG)
+                    s = jnp.where(edge_masks(zz, off_edge)[0], s, NEG)
                 sbuf[par, i] = s
                 new_tops.append((old, jnp.maximum(old, jnp.max(s, axis=0, keepdims=True))))
             if cur is not None:
@@ -244,7 +246,7 @@
         def _():
             zz = unit_z(k)
             kb, vb = keys_of(zz, x, 1)
-            s = jnp.where(edge_masks(zz)[1], nt(kb, qm[1]), NEG)
+            s = jnp.where(edge_masks(zz, zz < 0)[1], nt(kb, qm[1]), NEG)
             old = top[1]
             new = jnp.maximum(old, jnp.max(s, axis=0, keepdims=True))
             p = jnp.exp(s - new)

time: 83.2 us -> 82.7 us (level)
  no operation moved by 1% of the time
where the time goes in v5:
time: 82.7 us; the launch traced here: 82.6 us
  Pallas kernels  79.6 us (96%)
  local copies, waits for them, and re-layouts  2.3 us (3%)
    pallas_call x1, Pallas kernels, body(): pl.pallas_call(kernel, out_shape=(jax.ShapeDtypeStruct((2, R, 128), BF),)...  79.6 us
    unnamed x4, local copies, waits for them, and re-layouts  2.3 us

profile of v5, /device:TPU:1, one launch (start us, length us, event | category | flops | bytes accessed | tf_op | source)
XLA Modules:
  0.0 82.6 jit_solution(12214624693746871669)
XLA Ops:
  0.6 79.6 %shard_map.77 = (bf16[2,256,128]{2,1,0:T(8,128)(2,1)}, bf16[2,256,128]{2,1,0:T(8,128)(2,1)}) custom-call(bf16[2,256,128]{2,1,0:T(8,128)(2,1)} %bitcast.13, bf16[2,64,128]{2,1,0:T(8,128)(2,1)} %bitcast.15, bf16[2,64,128]{2,1,0:T(8,128)(2,1)} %bitcast.16, f32[4]{0:T(128)} %lam_ref.1, f32[1,128]{1,0:T(1,128)} %bitcast.17, bf16[2,256,128]{2,1,0:T(8,128)(2,1)} %bitcast.14), custom_call_target="tpu_custom_call" | custom-call | flops 12999999488 | bytes 2097152 | tf_op jit(solution)/shard_map/pallas_call | solution.py:444
  80.3 0.0 copy-start
  80.3 1.6 %copy.12 = bf16[2,1,1,64,4,128]{5,4,3,2,1,0:T(4,128)(2,1)} copy(bf16[2,1,1,64,4,128]{5,4,3,2,1,0:T(4,128)(2,1)} %bitcast.12) | data formatting | bytes 262144
  81.9 0.0 copy-done
  81.9 0.7 copy.13
Async XLA Ops:
  80.3 1.7 %copy-start = (bf16[2,256,128]{2,1,0:T(8,128)(2,1)S(1)}, bf16[2,256,128]{2,1,0:T(8,128)(2,1)}, u32[]{:S(2)}) copy-start(bf16[2,256,128]{2,1,0:T(8,128)(2,1)} %get-tuple-element.5) | copy-start | bytes 393220
